TPU v7x, 768 devices: a whole 4x8x12 slice. The times are simulated.
768 devices in a mesh: grp: 16 (over y, core), mem: 48 (over z, x).
Axes of the slice: x: 4, y: 8, z: 12, core: 2. Of those that a mesh axis runs over, the one named last changes fastest.
Arguments:
- points: float32 [196608, 1024], P(('grp', 'mem')), may hold values from -6 to 6
- owner: int32 [196608, 1], P(('grp', 'mem')), may hold values from 0 to 47; in each aligned block of 256 rows (0 to 255, 256 to 511, ...) at most 16 rows name the same one
- slot: int32 [196608], P(('grp', 'mem')), may hold values from 0 to 511
- centroids1: bfloat16 [393216, 1024], P(('grp', 'mem')), may hold values from -6 to 6
- mass1: float32 [393216], P(('grp', 'mem')), may hold values from 0.5 to 16
- parent1: int32 [393216], P(('grp', 'mem')), may hold values from 0 to 767
- centroids2: float32 [768, 1024], P('mem'), may hold values from -6 to 6
- mass2: float32 [768], P('mem'), may hold values from 32 to 1024
- parent2: int32 [768], P('mem'), may hold values from 0 to 255
- centroids3: float32 [256, 1024], replicated, may hold values from -6 to 6
- mass3: float32 [256], replicated, may hold values from 64 to 4096
Outputs:
- new1: bfloat16 [393216, 1024], P(('grp', 'mem'))
- new2: float32 [768, 1024], P('mem')
- new3: float32 [256, 1024], replicated
Inputs may be any that keep to these rules, and one draw needn't show every extreme that they name: Among the points of one device at most 16 name the same owner, and in every draw some device has exactly 16 points naming one owner.
All inputs are finite; a program needn't handle non-finite values.
Results may differ from a plain program's by a relative error of at most 0.004.
Values may be sent and summed in bfloat16 or wider, within the bound.
No kernel may reach another device: no remote copies, remote signals or barrier semaphores. Data moves between devices by JAX's collectives and lax.ppermute only.
A program may use at most 32 MiB of HBM per device.

v0:
```python
import jax
import jax.numpy as jnp
from jax import lax
from jax.sharding import PartitionSpec as P


def update_rows(sums, counts, olds, masses):
    return (sums + masses[:, None] * olds) / (counts + masses)[:, None]


def level_sums(row_ids, parents, sums, counts):
    pick = (row_ids[:, None] == parents[None, :]).astype(jnp.float32)
    part = jnp.dot(pick, sums, precision=lax.Precision.HIGHEST, preferred_element_type=jnp.float32)
    weight = jnp.dot(
        pick, counts, precision=lax.Precision.HIGHEST, preferred_element_type=jnp.float32
    )
    return (part, weight)


def local(
    points, owner, slot, centroids1, mass1, parent1, centroids2, mass2, parent2, centroids3, mass3
):
    rows, width = points.shape
    members = lax.axis_size("mem")
    capacity = 3 * rows // members
    local_count = centroids1.shape[0]
    per_member = centroids2.shape[0]
    total2 = per_member * members
    total3 = centroids3.shape[0]
    packed = points.astype(jnp.bfloat16)
    target = owner[:, 0]
    hits = (target[:, None] == jnp.arange(members)[None, :]).astype(jnp.int32)
    before = jnp.cumsum(hits, axis=0) - hits
    rank = jnp.sum(before * hits, axis=1)
    place = target * capacity + rank
    buffer = jnp.zeros((members * capacity, width), jnp.bfloat16).at[place].set(packed)
    labels = jnp.full((members * capacity,), -1, jnp.int32).at[place].set(slot)
    arrived, arrived_ids = (
        lax.all_to_all(
            buffer.reshape(members, capacity, width), "mem", split_axis=0, concat_axis=0, tiled=True
        ),
        lax.all_to_all(
            labels.reshape(members, capacity), "mem", split_axis=0, concat_axis=0, tiled=True
        ),
    )
    select = jnp.arange(local_count)[:, None] == arrived_ids.reshape(1, -1)
    sums1 = jnp.dot(
        select.astype(jnp.bfloat16), arrived.reshape(-1, width), preferred_element_type=jnp.float32
    )
    count1 = jnp.sum(select.astype(jnp.float32), axis=1)
    new1 = update_rows(sums1, count1, centroids1.astype(jnp.float32), mass1).astype(jnp.bfloat16)
    order = jnp.arange(total2, dtype=jnp.int32)
    part2, weight2 = level_sums(order, parent1, sums1, count1)
    group2, group_weight = (
        lax.psum_scatter(part2, "mem", scatter_dimension=0, tiled=True),
        lax.psum_scatter(weight2, "mem", scatter_dimension=0, tiled=True),
    )
    sums2, count2 = (
        lax.psum(group2.astype(jnp.bfloat16), "grp").astype(jnp.float32),
        lax.psum(group_weight.astype(jnp.bfloat16), "grp").astype(jnp.float32),
    )
    new2 = update_rows(sums2, count2, centroids2, mass2)
    ids3 = jnp.arange(total3, dtype=jnp.int32)
    part3, weight3 = level_sums(ids3, parent2, sums2, count2)
    sums3, count3 = lax.psum((part3, weight3), "mem")
    new3 = update_rows(sums3, count3, centroids3, mass3)
    return (new1, new2, new3)


def solution(mesh):
    placed = (
        P(("grp", "mem"), None),
        P(("grp", "mem"), None),
        P(("grp", "mem")),
        P(("grp", "mem"), None),
        P(("grp", "mem")),
        P(("grp", "mem")),
        P("mem", None),
        P("mem"),
        P("mem"),
        P(),
        P(),
    )
    return jax.shard_map(
        local,
        mesh=mesh,
        in_specs=placed,
        out_specs=(P(("grp", "mem"), None), P("mem", None), P()),
        check_vma=False,
    )
```

profile of v0, /device:TPU:1, one launch (start us, length us, event | category | flops | bytes accessed | tf_op | source)
XLA Modules:
  0.0 812.6 jit_solution(13965701285963810026)
XLA Ops:
  7.2 0.7 fusion.17
  7.9 0.6 reduce-window.6
  8.4 0.2 slice_reduce_fusion
  8.7 0.8 fusion.16
  9.5 0.7 compare_select_fusion
  10.1 1.6 scatter_custom_fusion
  11.7 0.7 all_to_all.9
  12.4 18.8 %all-to-all-start = ((s32[48,1,16]{2,1,0:T(1,128)}), s32[48,1,16]{2,1,0:T(1,128)S(1)}, u32[]{:S(2)}, u32[]{:S(2)}) async-start(s32[48,1,16]{2,1,0:T(1,128)} %bitcast.5), calls=%async_computation | async-start | bytes 49152 | tf_op jit(solution)/shard_map/all_to_all | solution.py:42
  31.2 3.6 scatter_custom_fusion.1
  34.9 7.2 all-to-all-done
  42.1 4.8 all-to-all-start.1
  46.9 0.5 broadcast.44
  47.5 0.7 reduce.7
  48.2 0.1 eq.75
  48.3 0.2 convert_reduce_fusion
  48.5 52.3 %all-to-all-done.1 = bf16[48,16,1024]{2,1,0:T(8,128)(2,1)S(1)} async-done(((bf16[48,16,1024]{2,1,0:T(8,128)(2,1)}), bf16[48,16,1024]{2,1,0:T(8,128)(2,1)S(1)}, u32[]{:S(2)}, u32[]{:S(2)}) %all-to-all-start.1) | async-done | bytes 1572896 | tf_op jit(solution)/shard_map/all_to_all | solution.py:39
  100.8 2.0 divide_convert_fusion
  102.8 4.4 fusion.1
  107.3 0.0 all-reduce.4.cloned.1.call-start
  107.4 1.4 dynamic-slice
  109.4 0.8 fusion.3
  110.2 87.7 %all-reduce = bf16[768]{0:T(1024)(128)(2,1)S(1)} all-reduce(f32[768]{0:T(1024)S(1)} %fusion.3), channel_id=3, replica_groups=mesh['grp'=16,'mem'=48] {'mem'}, use_global_device_ids=true, to_apply=%region_8.9.clone | all-reduce | flops 768 | bytes 4608
  197.9 0.1 dynamic-slice.3
  198.0 332.9 %reduce-scatter.2.cloned.1.call-done = f32[16,1024]{1,0:T(8,128)} async-done(((f32[768,1024]{1,0:T(8,128)}), f32[16,1024]{1,0:T(8,128)}) %reduce-scatter.2.cloned.1.call-update) | async-done | bytes 65552 | tf_op jit(solution)/shard_map/reduce_scatter | solution.py:55
  530.9 0.8 convert_element_type.40
  531.7 51.6 %all-reduce.1 = (bf16[16,1024]{1,0:T(8,128)(2,1)S(1)}, bf16[16]{0:T(256)(128)(2,1)S(1)}) all-reduce(bf16[16,1024]{1,0:T(8,128)(2,1)S(1)} %convert_element_type.40, bf16[16]{0:T(256)(128)(2,1)S(1)} %dynamic-slice.3), channel_id=1, replica_groups=mesh['grp'=16,'mem'=48] {'grp'}, use_global_device_ids=true, to_apply=%region_7.8 | all-reduce | flops 16400 | bytes 65600 | tf_op jit(solution)/shard_map/psum | solution.py:59
  583.3 1.2 fusion.11
  584.6 0.1 fusion.10
  584.7 85.8 %psum.31 = f32[256]{0:T(256)S(1)} all-reduce(f32[256]{0:T(256)S(1)} %bitcast.45), channel_id=1, replica_groups=mesh['grp'=16,'mem'=48] {'mem'}, use_global_device_ids=true, to_apply=%region_11.12 | all-reduce | flops 256 | bytes 2048 | tf_op jit(solution)/shard_map/psum | solution.py:65
  670.5 0.7 add_divide_fusion.1
  671.2 132.1 %all-reduce.4.cloned.1.call-done = f32[256,1024]{1,0:T(8,128)} async-done(((f32[256,1024]{1,0:T(8,128)}), f32[256,1024]{1,0:T(8,128)}) %all-reduce.4.cloned.1.call-update) | async-done | bytes 1048592 | tf_op jit(solution)/shard_map/psum | solution.py:65
  803.4 2.4 add_divide_fusion
  (24 shorter events, 0.2 us)
Async XLA Ops:
  12.4 29.7 %all-to-all-start = ((s32[48,1,16]{2,1,0:T(1,128)}), s32[48,1,16]{2,1,0:T(1,128)S(1)}, u32[]{:S(2)}, u32[]{:S(2)}) async-start(s32[48,1,16]{2,1,0:T(1,128)} %bitcast.5), calls=%async_computation | async-start | bytes 49152 | tf_op jit(solution)/shard_map/all_to_all | solution.py:42
  42.1 6.4 copy-start.4
  42.1 58.7 %copy-start.7 = (bf16[512,1024]{1,0:T(8,128)(2,1)S(1)}, bf16[512,1024]{1,0:T(8,128)(2,1)}, u32[]{:S(2)}) copy-start(bf16[512,1024]{1,0:T(8,128)(2,1)} %param.14) | copy-start | bytes 3145732
  42.1 58.7 %all-to-all-start.1 = ((bf16[48,16,1024]{2,1,0:T(8,128)(2,1)}), bf16[48,16,1024]{2,1,0:T(8,128)(2,1)S(1)}, u32[]{:S(2)}, u32[]{:S(2)}) async-start(bf16[48,16,1024]{2,1,0:T(8,128)(2,1)} %bitcast.6), calls=%async_computation.1 | async-start | bytes 3145728 | tf_op jit(solution)/shard_map/all_to_all | solution.py:39
  46.9 484.0 %reduce-scatter.2.cloned.1.call-start = ((), (), s32[]{:S(2)}) async-start(), calls=%async_computation.3 | async-start | bytes 3211264 | tf_op jit(solution)/shard_map/reduce_scatter | solution.py:55
  100.8 2.0 copy-start.3
  107.3 476.0 %copy-start.5 = (s32[16]{0:T(128)S(1)}, s32[16]{0:T(128)}, u32[]{:S(2)}) copy-start(s32[16]{0:T(128)} %param.19) | copy-start | bytes 196
  107.3 563.2 %copy-start.2 = (f32[256]{0:T(256)S(1)}, f32[256]{0:T(256)}, u32[]{:S(2)}) copy-start(f32[256]{0:T(256)} %param.21) | copy-start | bytes 3076
  107.3 563.2 %copy-start.6 = (f32[16]{0:T(128)S(1)}, f32[16]{0:T(128)}, u32[]{:S(2)}) copy-start(f32[16]{0:T(128)} %param.18) | copy-start | bytes 196
  107.3 563.2 %copy-start.1 = (f32[16,1024]{1,0:T(8,128)S(1)}, f32[16,1024]{1,0:T(8,128)}, u32[]{:S(2)}) copy-start(f32[16,1024]{1,0:T(8,128)} %param.17) | copy-start | bytes 196612
  107.3 696.0 %copy-start = (f32[256,1024]{1,0:T(8,128)S(1)}, f32[256,1024]{1,0:T(8,128)}, u32[]{:S(2)}) copy-start(f32[256,1024]{1,0:T(8,128)} %param.20) | copy-start | bytes 3145732
  107.3 696.0 %all-reduce.4.cloned.1.call-start = ((), (), s32[]{:S(2)}) async-start(), calls=%async_computation.4 | async-start | bytes 2097152 | tf_op jit(solution)/shard_map/psum | solution.py:65
Sparse Core Ops, SparseCore 0:
  107.4 423.4 reduce-scatter.1
  584.7 218.6 all-reduce.3
where the time goes:
time: 819 us; the launch traced here: 813 us
  waiting for transfers between devices  525 us (64%)
  blocking collectives  225 us (27%)
  starting transfers between devices  23.7 us (3%)
  between operations  14.8 us (2%)
  other arithmetic  11.3 us (1%)
  matrix products  8.66 us (1%)
    reduce_scatter x1, waiting for transfers between devices, local(): lax.psum_scatter(part2, 'mem', scatter_dimension=0, tiled=True)  333 us
    psum x1, waiting for transfers between devices, local(): sums3, count3 = lax.psum((part3, weight3), 'mem')  132 us
    unnamed x1, blocking collectives  87.7 us
    psum x1, blocking collectives, local(): sums3, count3 = lax.psum((part3, weight3), 'mem')  85.8 us
    all_to_all x1, waiting for transfers between devices, local(): lax.all_to_all(buffer.reshape(members, capacity, width), 'mem', split_axi...  52.3 us
    psum x1, blocking collectives, local(): lax.psum(group2.astype(jnp.bfloat16), 'grp').astype(jnp.float32)  51.6 us
    all_to_all x1, starting transfers between devices, local(): lax.all_to_all(labels.reshape(members, capacity), 'mem', split_axis=0, co...  18.8 us
  transfers between devices with their start and end apart: 4, of which 4 were waited for; matrix products, arithmetic and copies ran while one was open for 1% of the time, Pallas kernels for 0%

commit v1 on v0

v1 whole, which is shorter than its diff:
```python
import jax
import jax.numpy as jnp
from jax import lax
from jax.experimental import pallas as pl
from jax.experimental.pallas import tpu as pltpu
from jax.sharding import Mesh
from jax.sharding import PartitionSpec as P

BF16, F32, I32 = jnp.bfloat16, jnp.float32, jnp.int32
CORES, XS, LANES, CAP, EXTRA = 2, 4, 128, 16, 16
TILES = CORES * XS
ROOM = 32 * 1024 * 1024
MASKS = (1, 2, 6)


def coded(y):
    return y ^ (((y >> 2) & 1) << 1)


def iota(shape, dim):
    return lax.broadcasted_iota(I32, shape, dim)


def dot(a, b, contract=((1,), (0,))):
    return lax.dot_general(a, b, (contract, ((), ())), preferred_element_type=F32)


def column(row):
    eye = iota((LANES, LANES), 0) == iota((LANES, LANES), 1)
    return jnp.sum(jnp.where(eye, row, 0.0), axis=1, keepdims=True)


def encode(counts):
    whole = counts.astype(I32)
    row = iota((EXTRA, LANES), 0)
    parts = jnp.where(row == 0, whole & 0x7FFF0000, jnp.where(row == 1, whole & 0xFF00, whole & 0xFF))
    return jnp.where(row < 3, parts, 0).astype(F32).astype(BF16)


def decode(tile):
    return jnp.sum(tile[0:3].astype(F32), axis=0, keepdims=True)


def ranks(own, members):
    rows = own.shape[1]
    hit = iota((members, rows), 0) == own
    earlier = (iota((rows, rows), 0) < iota((rows, rows), 1)).astype(BF16)
    before = dot(hit.astype(BF16), earlier)
    return jnp.sum(jnp.where(hit, before, 0.0), axis=0, keepdims=True).astype(I32), hit


def table_kernel(owner, slot, parent1, parent2, table, *scratch):
    held, sems = scratch[:-1], scratch[-1]
    copies = [
        pltpu.make_async_copy(src, dst, sems.at[i])
        for i, (src, dst) in enumerate(zip((owner, slot, parent1, parent2), held))
    ]
    for copy in copies:
        copy.start()
    for copy in copies:
        copy.wait()
    owner, slot, parent1, parent2 = held
    members, rows, per = table.shape[0], owner.shape[1], parent2.shape[1]
    place = slot[...]
    rank, hit = ranks(owner[...], members)
    code = jnp.where(place < 256, place + 1, 255 - place).astype(F32)
    spread = (iota((LANES, rows), 0) == per + rank).astype(BF16)
    codes = dot(jnp.where(hit, code, 0.0).astype(BF16), spread, ((1,), (1,)))
    slots = jnp.where(codes > 0, codes - 1, jnp.where(codes < 0, 255 - codes, -1.0)).astype(I32)
    lines = parent1.shape[0]
    row, lane = iota((8, LANES), 0), iota((8, LANES), 1)
    known = jnp.concatenate([parent1[...], jnp.zeros((8 - lines, LANES), I32)], axis=0)
    level2 = jnp.concatenate([parent2[...], jnp.zeros((1, LANES - per), I32)], axis=1)
    known = jnp.where((row == lines) & (lane < per), level2, known)
    for m in range(members):
        table[m] = jnp.where((row == lines) & (lane >= per), slots[m : m + 1, :], known)


def pack_kernel(points, owner, send, rounded):
    rows, members = points.shape[0], send.shape[0]
    rounded[...] = points[...].astype(BF16)
    own = owner[...]
    rank, _ = ranks(own, members)
    pick = (iota((members * CAP, rows), 0) == own * CAP + rank).astype(BF16)
    for pair in range(TILES // 2):
        moved = dot(pick, rounded[:, pair * 2 * LANES : (pair + 1) * 2 * LANES]).astype(BF16)
        for half in range(2):
            tile = moved[:, half * LANES : (half + 1) * LANES].reshape(members, CAP, LANES)
            start = (2 * pair + half) * CAP
            send[:, start : start + CAP, :] = tile


def look_kernel(at, table, owner, slot, rounded, keep, swap):
    core, x = at[0], at[1]
    rows, members = rounded.shape[0], table.shape[0]
    lines = rows // LANES
    hit = (iota((members, rows), 0) == owner[...]).astype(BF16)
    parent = jnp.zeros((1, rows), F32)
    for j in range(4):
        known = table[:, j, :]
        high = (known >> 8).astype(F32).astype(BF16)
        low = (known & 255).astype(F32).astype(BF16)
        found = dot(high, hit, ((0,), (0,))) * 256.0 + dot(low, hit, ((0,), (0,)))
        here = iota((LANES, rows), 0) + j * LANES == slot[...]
        parent += jnp.sum(jnp.where(here, found, 0.0), axis=0, keepdims=True)
    whole = parent.astype(I32)
    parts = [v[:, i * LANES : (i + 1) * LANES] for v in (whole >> 8, whole & 255) for i in range(lines)]
    notes = jnp.zeros((EXTRA, LANES), I32)
    for i, v in enumerate(parts):
        notes = jnp.where(iota((EXTRA, LANES), 0) == i, v, notes)
    notes = notes.astype(F32).astype(BF16)
    for out, to in ((keep, core), (swap, 1 - core)):
        for k in range(XS):
            start = pl.multiple_of((to * XS + ((x + k) & (XS - 1))) * LANES, LANES)
            out[k, 0:rows, :] = rounded[:, pl.ds(start, LANES)]
            out[k, rows : rows + EXTRA, :] = notes


def join_kernel(mine, other, *outs):
    for k in range(1, XS):
        outs[k - 1][0] = mine[k]
        outs[k - 1][1] = other[k]


def part_kernel(at, *refs):
    blocks, (keep, send, total) = refs[:-3], refs[-3:]
    rows = blocks[0].shape[1] - EXTRA
    lines = rows // LANES
    cents = total.shape[0]
    per_y = keep.shape[1] - EXTRA
    ones = jnp.ones((rows, LANES), BF16)
    for s in range(TILES):
        block = blocks[s].at[0] if s < 2 else blocks[2 + (s - 2) // 2].at[s % 2]
        notes = block[rows : rows + EXTRA, :].astype(F32)
        parent = jnp.concatenate(
            [notes[i : i + 1] * 256.0 + notes[lines + i : lines + i + 1] for i in range(lines)], axis=1
        ).astype(I32)
        pick = (iota((cents, rows), 0) == parent).astype(BF16)
        part = dot(pick, jnp.concatenate([block[0:rows, :], ones], axis=1))
        if s == 0:
            total[...] = part
        else:
            total[...] += part
    diagonal = iota((per_y, LANES), 0) == iota((per_y, LANES), 1)
    for i in range(keep.shape[0]):
        for out, bit in ((keep, at[0]), (send, 1 - at[0])):
            start = pl.multiple_of((2 * i + bit) * per_y, 16)
            counts = total[pl.ds(start, per_y), LANES : 2 * LANES]
            row = jnp.sum(jnp.where(diagonal, counts, 0.0), axis=0, keepdims=True)
            out[i, 0:per_y, :] = total[pl.ds(start, per_y), 0:LANES].astype(out.dtype)
            out[i, per_y : per_y + EXTRA, :] = encode(row).astype(out.dtype)


def write(out, i, total):
    per_y = total.shape[0] - EXTRA
    out[i, 0:per_y, :] = total[0:per_y].astype(out.dtype)
    out[i, per_y : per_y + EXTRA, :] = encode(decode(total[per_y:])).astype(out.dtype)


def halve_kernel(at, kept, came, keep, send):
    for i in range(keep.shape[0]):
        for out, bit in ((keep, at[0]), (send, 1 - at[0])):
            j = 2 * i + bit
            write(out, i, kept[j] + came[j].astype(F32))


def last_kernel(kept, came, out):
    write(out, 0, kept[0] + came[0].astype(F32))


def add_kernel(blocks, out):
    total = blocks[0].astype(F32)
    for i in range(1, blocks.shape[0]):
        total = total + blocks[i].astype(F32)
    for i in range(out.shape[0]):
        write(out, i, total)


def level3_kernel(at, held, parents, payload, count3, count2, sums2, counts2):
    z, x = at[0], at[1]
    ys, padded, _ = held.shape
    per_y = padded - EXTRA
    total3 = count3.shape[0]
    sums3 = jnp.zeros((total3, LANES), F32)
    counts3 = jnp.zeros((total3, LANES), F32)
    for y in range(ys):
        block, code = held[y], coded(y)
        row = decode(block[per_y : per_y + EXTRA])
        pick = iota((total3, LANES), 0) == parents[code : code + 1, :]
        counts3 += jnp.where(pick, row, 0.0)
        fill = jnp.zeros((LANES - per_y, LANES), BF16)
        sums3 += dot(
            pick.astype(BF16), jnp.concatenate([block[0:per_y], fill], axis=0)
        )
        sums2[code * per_y : (code + 1) * per_y, :] = block[0:per_y]
        counts2[code * per_y : (code + 1) * per_y, :] = jnp.broadcast_to(
            column(row)[0:per_y], (per_y, LANES)
        )
    count3[...] = jnp.broadcast_to(jnp.sum(counts3, axis=1, keepdims=True), count3.shape)
    start = pl.multiple_of((z * XS + x) * CAP, CAP)
    count2[...] = counts2[pl.ds(start, CAP), :]
    rounded = sums3.astype(BF16)
    for k in range(TILES):
        start = pl.multiple_of((z * XS + k % XS) * CAP, CAP)
        payload[k, 0:total3, :] = rounded
        payload[k, total3 : total3 + CAP, :] = sums2[pl.ds(start, CAP), :]


def top_kernel(held, count3, count2, cents3, mass3, cents2, mass2, new3, new2):
    total3, per = cents3.shape[0], cents2.shape[0]
    weight3 = jnp.concatenate([column(mass3[i : i + 1, :]) for i in range(total3 // LANES)], axis=0)
    weight2 = column(mass2[...])[0:per]
    scale3 = 1.0 / (count3[:, 0:1] + weight3)
    scale2 = 1.0 / (count2[:, 0:1] + weight2)
    for k in range(TILES):
        cols = slice(k * LANES, (k + 1) * LANES)
        new3[:, cols] = (held[k, 0:total3, :].astype(F32) + weight3 * cents3[:, cols]) * scale3
        new2[:, cols] = (
            held[k, total3 : total3 + per, :].astype(F32) + weight2 * cents2[:, cols]
        ) * scale2


def level1_kernel(arrived, place, cents1, mass1, new1):
    members = arrived.shape[0]
    local = cents1.shape[0]
    parts = [
        iota((local, LANES), 0) == place[i : i + 1, :] for i in range(members * CAP // LANES)
    ]
    counts = sum(v.astype(F32) for v in parts)
    counts = jnp.sum(counts, axis=1, keepdims=True)
    pick = jnp.concatenate([v.astype(BF16) for v in parts], axis=1)
    weight = jnp.concatenate([column(mass1[i : i + 1, :]) for i in range(local // LANES)], axis=0)
    scale = 1.0 / (counts + weight)
    for pair in range(TILES // 2):
        halves = [
            arrived[:, t * CAP : (t + 1) * CAP, :].reshape(members * CAP, LANES)
            for t in (2 * pair, 2 * pair + 1)
        ]
        sums = dot(pick, jnp.concatenate(halves, axis=1))
        cols = slice(pair * 2 * LANES, (pair + 1) * 2 * LANES)
        new1[:, cols] = ((sums + weight * cents1[:, cols].astype(F32)) * scale).astype(BF16)


SMEM = pl.BlockSpec(memory_space=pltpu.SMEM)
VMEM = pl.BlockSpec(memory_space=pltpu.VMEM)
HBM = pl.BlockSpec(memory_space=pltpu.HBM)


def call(kernel, outs, args, scalars=0, scratch=(), name=None, places=VMEM, room=ROOM):
    return pl.pallas_call(
        kernel,
        out_shape=outs,
        in_specs=[SMEM] * scalars + [places] * (len(args) - scalars),
        out_specs=jax.tree.map(lambda _: VMEM, outs),
        scratch_shapes=list(scratch),
        compiler_params=pltpu.CompilerParams(vmem_limit_bytes=room),
        name=name,
    )(*args)


def array(shape, dtype=BF16):
    return jax.ShapeDtypeStruct(shape, dtype)


def exchange(v, axes):
    return lax.all_to_all(v, axes, split_axis=0, concat_axis=0, tiled=True)


def local(
    points, owner, slot, centroids1, mass1, parent1, centroids2, mass2, parent2, centroids3, mass3
):
    rows = points.shape[0]
    ys, zs = lax.axis_size("y"), lax.axis_size("z")
    y, core, z, x = (lax.axis_index(a) for a in ("y", "core", "z", "x"))
    members = zs * XS
    per = centroids2.shape[0]
    total2, total3 = per * members, centroids3.shape[0]
    per_y = total2 // ys
    slots = centroids1.shape[0]

    owner, slot = owner.reshape(1, rows), slot.reshape(1, rows)
    small = [owner, slot, parent1.reshape(-1, LANES), parent2.reshape(1, per)]
    table = call(
        table_kernel,
        array((members, 8, LANES), I32),
        small,
        scratch=[pltpu.VMEM(v.shape, I32) for v in small] + [pltpu.SemaphoreType.DMA((len(small),))],
        name="tables",
        places=HBM,
        room=None,
    )
    send, rounded = call(
        pack_kernel,
        [array((members, TILES * CAP, LANES)), array(points.shape)],
        [points, owner],
        name="pack",
    )
    table = exchange(table, ("z", "x"))
    send, table = lax.optimization_barrier((send, table))
    arrived = exchange(send, ("z", "x"))

    kept, other = call(
        look_kernel,
        [array((XS, rows + EXTRA, LANES))] * 2,
        [jnp.stack([core, x]).astype(I32), table, owner, slot, rounded],
        scalars=1,
        name="look_up",
    )
    other = lax.ppermute(other, "core", [(0, 1), (1, 0)])
    joined = call(
        join_kernel, [array((2, rows + EXTRA, LANES))] * (XS - 1), [kept, other], name="join"
    )
    blocks = [kept, other] + [
        lax.ppermute(v, "x", [(i, (i + k) % XS) for i in range(XS)])
        for k, v in enumerate(joined, 1)
    ]

    parents2 = table[:, slots // LANES, 0:per].reshape(ys, per_y)
    parents2 = jnp.pad(parents2, ((0, 0), (0, LANES - per_y)), constant_values=-1)
    places = table[:, slots // LANES, per : per + CAP].reshape(-1, LANES)
    spot = jnp.stack([z, x]).astype(I32)

    def pair(count):
        return [array((count, per_y + EXTRA, LANES), dtype) for dtype in (F32, BF16)]

    count, bit = ys // 2, 0
    kept, going = call(
        part_kernel,
        pair(count),
        [(y & 1).reshape(1).astype(I32), *blocks],
        scalars=1,
        scratch=[pltpu.VMEM((total2, 2 * LANES), F32)],
        name="level2_parts",
    )
    going, parents2, places, spot = lax.optimization_barrier((going, parents2, places, spot))
    while True:
        came = lax.ppermute(going, "y", [(i, i ^ MASKS[bit]) for i in range(ys)])
        if count == 1:
            break
        count, bit = count // 2, bit + 1
        kept, going = call(
            halve_kernel,
            pair(count),
            [((coded(y) >> bit) & 1).reshape(1).astype(I32), kept, came],
            scalars=1,
            name="halve",
        )
    mine = call(
        last_kernel, array((1, per_y + EXTRA, LANES)), [kept, came], name="add_over_y"
    )
    whole = lax.all_gather(mine, "z", tiled=True)
    known = call(
        add_kernel, array((ys, per_y + EXTRA, LANES)), [whole], name="add_over_z"
    )
    known, arrived = lax.optimization_barrier((known, arrived))
    known = exchange(known, "y")

    payload, count3, count2 = call(
        level3_kernel,
        [array((TILES, total3 + CAP, LANES)), array((total3, LANES), F32), array((per, LANES), F32)],
        [spot, known, parents2],
        scalars=1,
        scratch=[pltpu.VMEM((total2, LANES), BF16), pltpu.VMEM((total2, LANES), F32)],
        name="level3_sums",
    )
    payload, arrived = lax.optimization_barrier((payload, arrived))
    payload = exchange(payload, ("core", "x"))
    new3, new2 = call(
        top_kernel,
        [array(centroids3.shape, F32), array(centroids2.shape, F32)],
        [
            payload,
            count3,
            count2,
            centroids3,
            mass3.reshape(-1, LANES),
            centroids2,
            jnp.pad(mass2, (0, LANES - per)).reshape(1, LANES),
        ],
        name="new3_new2",
    )
    new1 = call(
        level1_kernel,
        array(centroids1.shape),
        [arrived, places, centroids1, mass1.reshape(-1, LANES)],
        name="new1",
    )
    return (new1, new2, new3)


def solution(mesh):
    grp, mem = mesh.devices.shape
    shape = (grp // CORES, CORES, mem // XS, XS)
    fine = Mesh(mesh.devices.reshape(shape), ("y", "core", "z", "x"))
    both, zx = P(("y", "core", "z", "x")), P(("z", "x"))
    placed = (both,) * 6 + (zx,) * 3 + (P(),) * 2
    return jax.shard_map(
        local,
        mesh=fine,
        in_specs=placed,
        out_specs=(both, zx, P()),
        check_vma=False,
    )
```

time: 819 us -> 150 us (0.18)
  waiting for transfers between devices: 525 us -> 28 us
  blocking collectives: 225 us -> 40.3 us
  starting transfers between devices: 23.7 us -> 64.9 us
  between operations: 14.8 us -> 0.84 us
  Pallas kernels: 0 us -> 11.3 us
  other arithmetic: 11.3 us -> 0.15 us
  matrix products: 8.66 us -> 0 us
    reduce_scatter x1 -> x0, waiting for transfers between devices: 333 us -> none  [local(): lax.psum_scatter(part2, 'mem', scatter_dimension=0, tiled=True)]
    psum x2 -> x0, blocking collectives: 137 us -> none  [the longest x1 85.8 us: local(): sums3, count3 = lax.psum((part3, weight3), 'mem')]
    psum x1 -> x0, waiting for transfers between devices: 132 us -> none  [local(): sums3, count3 = lax.psum((part3, weight3), 'mem')]
    unnamed x1 -> x0, blocking collectives: 87.7 us -> none
    all_to_all x2 -> x3, waiting for transfers between devices: 59.5 us -> 16.4 us  [exchange(): return lax.all_to_all(v, axes, split_axis=0, concat_axis=0, tiled=True)]
    ppermute x0 -> x7, starting transfers between devices: none -> 27.5 us  [the longest x3 13.3 us: local(): came = lax.ppermute(going, 'y', [(i, i ^ MASKS[bit]) for i in range(ys)])]
    all_gather x0 -> x1, blocking collectives: none -> 24.7 us  [local(): whole = lax.all_gather(mine, 'z', tiled=True)]
    all_to_all x0 -> x1, blocking collectives: none -> 15.6 us  [exchange(): return lax.all_to_all(v, axes, split_axis=0, concat_axis=0, tiled=True)]
  transfers between devices with their start and end apart: 4 -> 10, of which waited for: 4 -> 8; matrix products, arithmetic and copies ran while one was open for 1% -> 0% of each run, Pallas kernels for 0% -> 4%
where the time goes in v1:
time: 150 us; the launch traced here: 149 us
  starting transfers between devices  64.9 us (43%)
  blocking collectives  40.3 us (27%)
  waiting for transfers between devices  28 us (19%)
  Pallas kernels  11.3 us (8%)
  local copies, waits for them, and re-layouts  3.5 us (2%)
    all_to_all x3, starting transfers between devices, exchange(): return lax.all_to_all(v, axes, split_axis=0, concat_axis=0, tiled=True)  37.4 us
    all_gather x1, blocking collectives, local(): whole = lax.all_gather(mine, 'z', tiled=True)  24.7 us
    all_to_all x3, waiting for transfers between devices, exchange(): return lax.all_to_all(v, axes, split_axis=0, concat_axis=0, tiled=True)  16.4 us
    all_to_all x1, blocking collectives, exchange(): return lax.all_to_all(v, axes, split_axis=0, concat_axis=0, tiled=True)  15.6 us
    ppermute x3, starting transfers between devices, local(): came = lax.ppermute(going, 'y', [(i, i ^ MASKS[bit]) for i in range(ys)])  13.3 us
    pallas_call x12, Pallas kernels, call(): pl.pallas_call(kernel, out_shape=outs, in_specs=[SMEM] * scalars + [place...  11.3 us
    ppermute x3, starting transfers between devices, local(): lax.ppermute(v, 'x', [(i, (i + k) % XS) for i in range(XS)])  10.7 us
    ppermute x3, waiting for transfers between devices, local(): came = lax.ppermute(going, 'y', [(i, i ^ MASKS[bit]) for i in range(ys)])  6.03 us
  transfers between devices with their start and end apart: 10, of which 8 were waited for; matrix products, arithmetic and copies ran while one was open for 0% of the time, Pallas kernels for 4%

profile of v1, /device:TPU:1, one launch (start us, length us, event | category | flops | bytes accessed | tf_op | source)
XLA Modules:
  0.0 149.0 jit_solution(8816532244902825504)
XLA Ops:
  0.6 1.8 %tables.1 = s32[48,8,128]{2,1,0:T(8,128)} custom-call(s32[1,256]{1,0:T(1,128)} %bitcast.14, s32[1,256]{1,0:T(1,128)} %bitcast.17, s32[4,128]{1,0:T(4,128)} %bitcast.21, s32[1,16]{1,0:T(1,128)} %bitcast.22), custom_call_target="tpu_custom_call" | custom-call | tf_op jit(solution)/shard_map/tables/pallas_call | solution.py:250
  2.4 18.9 %all-to-all-start = ((s32[48,8,128]{2,1,0:T(8,128)}), s32[48,8,128]{2,1,0:T(8,128)S(1)}, u32[]{:S(2)}, u32[]{:S(2)}) async-start(s32[48,8,128]{2,1,0:T(8,128)} %tables.1), calls=%async_computation | async-start | bytes 393216 | tf_op jit(solution)/shard_map/all_to_all | solution.py:266
  21.3 1.2 copy-done
  22.5 0.7 copy-done.4
  23.2 1.9 %pack.1 = (bf16[48,128,128]{2,1,0:T(8,128)(2,1)}, bf16[256,1024]{1,0:T(8,128)(2,1)S(1)}) custom-call(f32[256,1024]{1,0:T(8,128)S(1)} %copy-done, s32[1,256]{1,0:T(1,128)S(1)} %bitcast.15), custom_call_target="tpu_custom_call" | custom-call | tf_op jit(solution)/shard_map/pack/pallas_call | solution.py:250
  25.1 10.1 %all-to-all-done.table = s32[48,8,128]{2,1,0:T(8,128)S(1)} async-done(((s32[48,8,128]{2,1,0:T(8,128)}), s32[48,8,128]{2,1,0:T(8,128)S(1)}, u32[]{:S(2)}, u32[]{:S(2)}) %all-to-all-start) | async-done | bytes 196640 | tf_op jit(solution)/shard_map/all_to_all | solution.py:266
  35.2 6.1 %all-to-all-start.1 = ((bf16[48,128,128]{2,1,0:T(8,128)(2,1)}), bf16[48,128,128]{2,1,0:T(8,128)(2,1)S(1)}, u32[]{:S(2)}, u32[]{:S(2)}) async-start(bf16[48,128,128]{2,1,0:T(8,128)(2,1)} %get-tuple-element.47), calls=%async_computation.1 | async-start | bytes 3145728 | tf_op jit(solution)/shard_map/all_to_all | solution.py:266
  41.4 1.1 look_up.1
  42.6 3.5 %collective-permute-start = (bf16[4,272,128]{2,1,0:T(8,128)(2,1)S(1)}, bf16[4,272,128]{2,1,0:T(8,128)(2,1)S(1)}, u32[]{:S(2)}, u32[]{:S(2)}) collective-permute-start(bf16[4,272,128]{2,1,0:T(8,128)(2,1)S(1)} %get-tuple-element.35), channel_id=1, source_target_pairs={{0,48},{48,0},{1,49},{49,1},{2,50},{50,2},{3,51},{51,3},{4,52},{52... | collective-permute-start | bytes 835592 | tf_op jit(solution)/shard_map/ppermute | solution.py:309
  46.1 1.2 collective-permute-done.other.refs_1_
  47.3 3.3 %collective-permute-start.1 = (bf16[2,272,128]{2,1,0:T(8,128)(2,1)S(1)}, bf16[2,272,128]{2,1,0:T(8,128)(2,1)S(1)}, u32[]{:S(2)}, u32[]{:S(2)}) collective-permute-start(bf16[2,272,128]{2,1,0:T(8,128)(2,1)S(1)} %get-tuple-element.36), channel_id=1, source_target_pairs={{0,1},{1,2},{2,3},{3,0},{4,5},{5,6},{6,7},{7,4},{8,9},{9,10},{10,1... | collective-permute-start | bytes 417800 | tf_op jit(solution)/shard_map/ppermute | solution.py:314
  50.6 4.3 %collective-permute-start.2 = (bf16[2,272,128]{2,1,0:T(8,128)(2,1)S(1)}, bf16[2,272,128]{2,1,0:T(8,128)(2,1)S(1)}, u32[]{:S(2)}, u32[]{:S(2)}) collective-permute-start(bf16[2,272,128]{2,1,0:T(8,128)(2,1)S(1)} %get-tuple-element.37), channel_id=1, source_target_pairs={{0,2},{1,3},{2,0},{3,1},{4,6},{5,7},{6,4},{7,5},{8,10},{9,11},{10,... | collective-permute-start | bytes 417800 | tf_op jit(solution)/shard_map/ppermute | solution.py:314
  54.9 3.1 %collective-permute-start.3 = (bf16[2,272,128]{2,1,0:T(8,128)(2,1)S(1)}, bf16[2,272,128]{2,1,0:T(8,128)(2,1)S(1)}, u32[]{:S(2)}, u32[]{:S(2)}) collective-permute-start(bf16[2,272,128]{2,1,0:T(8,128)(2,1)S(1)} %get-tuple-element.38), channel_id=1, source_target_pairs={{0,3},{1,0},{2,1},{3,2},{4,7},{5,4},{6,5},{7,6},{8,11},{9,8},{10,9... | collective-permute-start | bytes 417800 | tf_op jit(solution)/shard_map/ppermute | solution.py:314
  58.0 0.1 pad_add_fusion.1.at
  58.1 0.2 slice_reduce_fusion
  58.5 2.4 %collective-permute-done.2.refs_3_ = bf16[2,272,128]{2,1,0:T(8,128)(2,1)S(1)} collective-permute-done((bf16[2,272,128]{2,1,0:T(8,128)(2,1)S(1)}, bf16[2,272,128]{2,1,0:T(8,128)(2,1)S(1)}, u32[]{:S(2)}, u32[]{:S(2)}) %collective-permute-start.2) | collective-permute-done | bytes 139296 | tf_op jit(solution)/shard_map/ppermute | solution.py:314
  60.8 2.0 %collective-permute-done.3.refs_4_ = bf16[2,272,128]{2,1,0:T(8,128)(2,1)S(1)} collective-permute-done((bf16[2,272,128]{2,1,0:T(8,128)(2,1)S(1)}, bf16[2,272,128]{2,1,0:T(8,128)(2,1)S(1)}, u32[]{:S(2)}, u32[]{:S(2)}) %collective-permute-start.3) | collective-permute-done | bytes 139296 | tf_op jit(solution)/shard_map/ppermute | solution.py:314
  62.8 1.0 level2_parts.1
  63.9 3.2 %collective-permute-start.4 = (bf16[4,112,128]{2,1,0:T(8,128)(2,1)S(1)}, bf16[4,112,128]{2,1,0:T(8,128)(2,1)S(1)}, u32[]{:S(2)}, u32[]{:S(2)}) collective-permute-start(bf16[4,112,128]{2,1,0:T(8,128)(2,1)S(1)} %get-tuple-element.42), channel_id=1, source_target_pairs={{0,96},{96,0},{192,288},{288,192},{384,480},{480,384},{576,672},{6... | collective-permute-start | bytes 344072 | tf_op jit(solution)/shard_map/ppermute | solution.py:337
  67.1 2.6 %collective-permute-done.4.came = bf16[4,112,128]{2,1,0:T(8,128)(2,1)S(1)} collective-permute-done((bf16[4,112,128]{2,1,0:T(8,128)(2,1)S(1)}, bf16[4,112,128]{2,1,0:T(8,128)(2,1)S(1)}, u32[]{:S(2)}, u32[]{:S(2)}) %collective-permute-start.4) | collective-permute-done | bytes 114720 | tf_op jit(solution)/shard_map/ppermute | solution.py:337
  69.8 4.2 %collective-permute-start.5 = (bf16[2,112,128]{2,1,0:T(8,128)(2,1)S(1)}, bf16[2,112,128]{2,1,0:T(8,128)(2,1)S(1)}, u32[]{:S(2)}, u32[]{:S(2)}) collective-permute-start(bf16[2,112,128]{2,1,0:T(8,128)(2,1)S(1)} %get-tuple-element.44), channel_id=1, source_target_pairs={{0,192},{96,288},{192,0},{288,96},{384,576},{480,672},{576,384},{6... | collective-permute-start | bytes 172040 | tf_op jit(solution)/shard_map/ppermute | solution.py:337
  74.0 1.9 %collective-permute-done.5.came = bf16[2,112,128]{2,1,0:T(8,128)(2,1)S(1)} collective-permute-done((bf16[2,112,128]{2,1,0:T(8,128)(2,1)S(1)}, bf16[2,112,128]{2,1,0:T(8,128)(2,1)S(1)}, u32[]{:S(2)}, u32[]{:S(2)}) %collective-permute-start.5) | collective-permute-done | bytes 57376 | tf_op jit(solution)/shard_map/ppermute | solution.py:337
  75.9 5.9 %collective-permute-start.6 = (bf16[1,112,128]{2,1,0:T(8,128)(2,1)S(1)}, bf16[1,112,128]{2,1,0:T(8,128)(2,1)S(1)}, u32[]{:S(2)}, u32[]{:S(2)}) collective-permute-start(bf16[1,112,128]{2,1,0:T(8,128)(2,1)S(1)} %get-tuple-element.46), channel_id=1, source_target_pairs={{0,576},{96,672},{192,384},{288,480},{384,192},{480,288},{576,0},{... | collective-permute-start | bytes 86024 | tf_op jit(solution)/shard_map/ppermute | solution.py:337
  81.8 1.5 %collective-permute-done.6.came = bf16[1,112,128]{2,1,0:T(8,128)(2,1)S(1)} collective-permute-done((bf16[1,112,128]{2,1,0:T(8,128)(2,1)S(1)}, bf16[1,112,128]{2,1,0:T(8,128)(2,1)S(1)}, u32[]{:S(2)}, u32[]{:S(2)}) %collective-permute-start.6) | collective-permute-done | bytes 28704 | tf_op jit(solution)/shard_map/ppermute | solution.py:337
  83.4 24.7 %all_gather.3.blocks = bf16[12,112,128]{2,1,0:T(8,128)(2,1)S(1)} all-gather(bf16[1,112,128]{2,1,0:T(8,128)(2,1)S(1)} %add_over_y.1), channel_id=1, replica_groups=mesh['y'=8,'core'=2,'z'=12,'x'=4] {'z'}, dimensions={0}, use_global_device_ids=true | all-gather | bytes 372736 | tf_op jit(solution)/shard_map/all_gather | solution.py:351
  108.1 15.6 %all_to_all.20.held = bf16[8,112,128]{2,1,0:T(8,128)(2,1)S(1)} all-to-all(bf16[8,112,128]{2,1,0:T(8,128)(2,1)S(1)} %add_over_z.1), channel_id=1, replica_groups=mesh['y'=8,'core'=2,'z'=12,'x'=4] {'y'}, dimensions={0} | all-to-all | bytes 458752 | tf_op jit(solution)/shard_map/all_to_all | solution.py:266
  123.7 1.7 %level3_sums.1 = (bf16[8,272,128]{2,1,0:T(8,128)(2,1)}, f32[256,128]{1,0:T(8,128)S(1)}, f32[16,128]{1,0:T(8,128)S(1)}) custom-call(s32[2]{0:T(128)S(1)} %pad_add_fusion.1.at, bf16[8,112,128]{2,1,0:T(8,128)(2,1)S(1)} %all_to_all.20.held, s32[8,128]{1,0:T(8,128)S(1)} %pad.8.parents), custom_call_target="tpu_custom_call" | custom-call | tf_op jit(solution)/shard_map/level3_sums/pallas_call | solution.py:250
  125.5 12.4 %all-to-all-start.3 = ((bf16[8,272,128]{2,1,0:T(8,128)(2,1)}), bf16[8,272,128]{2,1,0:T(8,128)(2,1)S(1)}, u32[]{:S(2)}, u32[]{:S(2)}) async-start(bf16[8,272,128]{2,1,0:T(8,128)(2,1)} %get-tuple-element.54), calls=%async_computation.3 | async-start | bytes 1114112 | tf_op jit(solution)/shard_map/all_to_all | solution.py:266
  137.9 1.2 copy-done.2
  139.1 2.2 %new1.1 = bf16[512,1024]{1,0:T(8,128)(2,1)} custom-call(bf16[48,128,128]{2,1,0:T(8,128)(2,1)S(1)} %all-to-all-done.1.arrived, s32[6,128]{1,0:T(8,128)S(1)} %reshape_squeeze.7.place, bf16[512,1024]{1,0:T(8,128)(2,1)S(1)} %copy-done.2, f32[4,128]{1,0:T(4,128)S(1)} %bitcast.19), custom_call_target="tpu_custom_call" | custom-call | tf_op jit(solution)/shard_map/new1/pallas_call | solution.py:250
  141.3 6.3 %all-to-all-done.3.held = bf16[8,272,128]{2,1,0:T(8,128)(2,1)S(1)} async-done(((bf16[8,272,128]{2,1,0:T(8,128)(2,1)}), bf16[8,272,128]{2,1,0:T(8,128)(2,1)S(1)}, u32[]{:S(2)}, u32[]{:S(2)}) %all-to-all-start.3) | async-done | bytes 557088 | tf_op jit(solution)/shard_map/all_to_all | solution.py:266
  147.6 1.3 new3_new2.1
  (29 shorter events, 0.5 us)
Async XLA Ops:
  2.4 32.8 %all-to-all-start = ((s32[48,8,128]{2,1,0:T(8,128)}), s32[48,8,128]{2,1,0:T(8,128)S(1)}, u32[]{:S(2)}, u32[]{:S(2)}) async-start(s32[48,8,128]{2,1,0:T(8,128)} %tables.1), calls=%async_computation | async-start | bytes 393216 | tf_op jit(solution)/shard_map/all_to_all | solution.py:266
  21.3 1.2 copy-start
  22.5 0.7 copy-start.4
  35.2 6.2 %copy-start.5 = (s32[256,1]{0,1:T(1,128)S(1)}, s32[256,1]{0,1:T(1,128)}, u32[]{:S(2)}) copy-start(s32[256,1]{0,1:T(1,128)} %param.12) | copy-start | bytes 3076
  35.2 6.2 %copy-start.6 = (s32[256]{0:T(256)S(1)}, s32[256]{0:T(256)}, u32[]{:S(2)}) copy-start(s32[256]{0:T(256)} %param.13) | copy-start | bytes 3076
  35.2 72.9 %all-to-all-start.1 = ((bf16[48,128,128]{2,1,0:T(8,128)(2,1)}), bf16[48,128,128]{2,1,0:T(8,128)(2,1)S(1)}, u32[]{:S(2)}, u32[]{:S(2)}) async-start(bf16[48,128,128]{2,1,0:T(8,128)(2,1)} %get-tuple-element.47), calls=%async_computation.1 | async-start | bytes 3145728 | tf_op jit(solution)/shard_map/all_to_all | solution.py:266
  42.6 4.7 %collective-permute-start = (bf16[4,272,128]{2,1,0:T(8,128)(2,1)S(1)}, bf16[4,272,128]{2,1,0:T(8,128)(2,1)S(1)}, u32[]{:S(2)}, u32[]{:S(2)}) collective-permute-start(bf16[4,272,128]{2,1,0:T(8,128)(2,1)S(1)} %get-tuple-element.35), channel_id=1, source_target_pairs={{0,48},{48,0},{1,49},{49,1},{2,50},{50,2},{3,51},{51,3},{4,52},{52... | collective-permute-start | bytes 835592 | tf_op jit(solution)/shard_map/ppermute | solution.py:309
  47.3 11.2 %collective-permute-start.1 = (bf16[2,272,128]{2,1,0:T(8,128)(2,1)S(1)}, bf16[2,272,128]{2,1,0:T(8,128)(2,1)S(1)}, u32[]{:S(2)}, u32[]{:S(2)}) collective-permute-start(bf16[2,272,128]{2,1,0:T(8,128)(2,1)S(1)} %get-tuple-element.36), channel_id=1, source_target_pairs={{0,1},{1,2},{2,3},{3,0},{4,5},{5,6},{6,7},{7,4},{8,9},{9,10},{10,1... | collective-permute-start | bytes 417800 | tf_op jit(solution)/shard_map/ppermute | solution.py:314
  50.6 10.2 %collective-permute-start.2 = (bf16[2,272,128]{2,1,0:T(8,128)(2,1)S(1)}, bf16[2,272,128]{2,1,0:T(8,128)(2,1)S(1)}, u32[]{:S(2)}, u32[]{:S(2)}) collective-permute-start(bf16[2,272,128]{2,1,0:T(8,128)(2,1)S(1)} %get-tuple-element.37), channel_id=1, source_target_pairs={{0,2},{1,3},{2,0},{3,1},{4,6},{5,7},{6,4},{7,5},{8,10},{9,11},{10,... | collective-permute-start | bytes 417800 | tf_op jit(solution)/shard_map/ppermute | solution.py:314
  54.9 7.9 %collective-permute-start.3 = (bf16[2,272,128]{2,1,0:T(8,128)(2,1)S(1)}, bf16[2,272,128]{2,1,0:T(8,128)(2,1)S(1)}, u32[]{:S(2)}, u32[]{:S(2)}) collective-permute-start(bf16[2,272,128]{2,1,0:T(8,128)(2,1)S(1)} %get-tuple-element.38), channel_id=1, source_target_pairs={{0,3},{1,0},{2,1},{3,2},{4,7},{5,4},{6,5},{7,6},{8,11},{9,8},{10,9... | collective-permute-start | bytes 417800 | tf_op jit(solution)/shard_map/ppermute | solution.py:314
  63.9 5.8 %collective-permute-start.4 = (bf16[4,112,128]{2,1,0:T(8,128)(2,1)S(1)}, bf16[4,112,128]{2,1,0:T(8,128)(2,1)S(1)}, u32[]{:S(2)}, u32[]{:S(2)}) collective-permute-start(bf16[4,112,128]{2,1,0:T(8,128)(2,1)S(1)} %get-tuple-element.42), channel_id=1, source_target_pairs={{0,96},{96,0},{192,288},{288,192},{384,480},{480,384},{576,672},{6... | collective-permute-start | bytes 344072 | tf_op jit(solution)/shard_map/ppermute | solution.py:337
  69.8 68.1 %copy-start.9 = (f32[16]{0:T(128)S(1)}, f32[16]{0:T(128)}, u32[]{:S(2)}) copy-start(f32[16]{0:T(128)} %param.18) | copy-start | bytes 196
  69.8 68.1 %copy-start.7 = (f32[512]{0:T(512)S(1)}, f32[512]{0:T(512)}, u32[]{:S(2)}) copy-start(f32[512]{0:T(512)} %param.15) | copy-start | bytes 6148
  69.8 6.1 %collective-permute-start.5 = (bf16[2,112,128]{2,1,0:T(8,128)(2,1)S(1)}, bf16[2,112,128]{2,1,0:T(8,128)(2,1)S(1)}, u32[]{:S(2)}, u32[]{:S(2)}) collective-permute-start(bf16[2,112,128]{2,1,0:T(8,128)(2,1)S(1)} %get-tuple-element.44), channel_id=1, source_target_pairs={{0,192},{96,288},{192,0},{288,96},{384,576},{480,672},{576,384},{6... | collective-permute-start | bytes 172040 | tf_op jit(solution)/shard_map/ppermute | solution.py:337
  75.9 7.4 %collective-permute-start.6 = (bf16[1,112,128]{2,1,0:T(8,128)(2,1)S(1)}, bf16[1,112,128]{2,1,0:T(8,128)(2,1)S(1)}, u32[]{:S(2)}, u32[]{:S(2)}) collective-permute-start(bf16[1,112,128]{2,1,0:T(8,128)(2,1)S(1)} %get-tuple-element.46), channel_id=1, source_target_pairs={{0,576},{96,672},{192,384},{288,480},{384,192},{480,288},{576,0},{... | collective-permute-start | bytes 86024 | tf_op jit(solution)/shard_map/ppermute | solution.py:337
  125.5 22.1 %all-to-all-start.3 = ((bf16[8,272,128]{2,1,0:T(8,128)(2,1)}), bf16[8,272,128]{2,1,0:T(8,128)(2,1)S(1)}, u32[]{:S(2)}, u32[]{:S(2)}) async-start(bf16[8,272,128]{2,1,0:T(8,128)(2,1)} %get-tuple-element.54), calls=%async_computation.3 | async-start | bytes 1114112 | tf_op jit(solution)/shard_map/all_to_all | solution.py:266
  137.9 1.2 copy-start.2
  139.1 8.5 %copy-start.1 = (f32[256,1024]{1,0:T(8,128)S(1)}, f32[256,1024]{1,0:T(8,128)}, u32[]{:S(2)}) copy-start(f32[256,1024]{1,0:T(8,128)} %cents3.1) | copy-start | bytes 3145732
  139.1 8.5 %copy-start.3 = (f32[16,1024]{1,0:T(8,128)S(1)}, f32[16,1024]{1,0:T(8,128)}, u32[]{:S(2)}) copy-start(f32[16,1024]{1,0:T(8,128)} %cents2.1) | copy-start | bytes 196612
  139.1 8.5 %copy-start.8 = (f32[256]{0:T(256)S(1)}, f32[256]{0:T(256)}, u32[]{:S(2)}) copy-start(f32[256]{0:T(256)} %param.21) | copy-start | bytes 3076
